TPU v7x, 32 devices: a whole 2x2x4 slice. The times are simulated.
32 devices in a mesh: dp: 4 (over x, core), seq: 8 (over z, y).
Axes of the slice: x: 2, y: 2, z: 4, core: 2. Of those that a mesh axis runs over, the one named last changes fastest.
Arguments:
- queries: bfloat16 [4, 1024, 4096], P('dp', 'seq'), may hold values from -2 to 2
- key_rows: bfloat16 [4, 1024, 4096], P('dp', 'seq'), may hold values from -2 to 2
- value_rows: bfloat16 [4, 1024, 4096], P('dp', 'seq'), may hold values from -6 to 6
- decay_rates: float32 [32], replicated, may hold values from 0 to 1, as said below
- norm_gain: float32 [4096], replicated, may hold values from 0.5 to 2
- reward_probe: float32 [4096], replicated, may hold values from -0.25 to 0.25
- step_ends: int32 [4, 64], P('dp'), may hold values from 0 to 1023, as said below
- step_counts: int32 [4, 64], P('dp'), may hold values from 0 to 8
Outputs:
- loss_total: float32 [], replicated
- grad_queries: bfloat16 [4, 1024, 4096], P('dp', 'seq')
- grad_keys: bfloat16 [4, 1024, 4096], P('dp', 'seq')
- grad_values: bfloat16 [4, 1024, 4096], P('dp', 'seq')
- grad_gain: float32 [4096], replicated
- grad_probe: float32 [4096], replicated
Inputs may be any that keep to these rules, and one draw needn't show every extreme that they name: `decay_rates`: positive rates. `step_ends`: within a pack the positions strictly increase, and the last one is 1023.
All inputs are finite; a program needn't handle non-finite values.
Results may differ from a plain program's by a relative error of at most 0.0094.
Values sent between devices are 32-bit elements; how exact they have to be, the bound alone decides.
A program may use at most 192 MiB of HBM per device.

v0:
```python
import jax
import jax.numpy as jnp
from jax import lax
from jax.sharding import PartitionSpec as P

STEPS = 64
ROLLOUTS = 8


loss_scaling = 32768.0
norm_epsilon = 1e-06


def prefix_2(part, axis, combine, identity, reverse):
    count = lax.axis_size(axis)
    place = lax.axis_index(axis)
    ahead = count - 1 - place if reverse else place
    gathered = jax.tree.map(lambda a: lax.all_gather(a, axis), part)
    state = jax.tree.map(lambda a, e: jnp.zeros_like(a) + jnp.asarray(e, a.dtype), part, identity)

    def one(hop, state):
        source = count - 1 - hop if reverse else hop
        return combine(
            state, jax.tree.map(lambda a: lax.dynamic_index_in_dim(a, source, 0, False), gathered)
        )

    return lax.fori_loop(0, ahead, one, state)


def combine_states(first_part, second_part):
    return (
        first_part[0] * second_part[0],
        second_part[0][:, None, None] * first_part[1] + second_part[1],
    )


def decay_tables(decay_rates, block_size):
    offsets = jnp.arange(block_size).astype(jnp.float32)
    gap = offsets[:, None] - offsets[None, :]
    causal = gap >= 0.0
    safe_gap = jnp.where(causal, gap, 0.0)
    within = jnp.where(causal[None], jnp.exp(-decay_rates[:, None, None] * safe_gap[None]), 0.0)
    rising = jnp.exp(-offsets[:, None] * decay_rates[None, :])
    falling = jnp.exp(-(block_size - offsets)[:, None] * decay_rates[None, :])
    return (within, rising, falling)


def on_device(
    queries, key_rows, value_rows, decay_rates, norm_gain, reward_probe, step_ends, step_counts
):
    head_count = decay_rates.shape[0]
    block_size = queries.shape[1]
    head_width = queries.shape[2] // head_count
    length = block_size * lax.axis_size("seq")
    query_heads = queries[0].reshape(block_size, head_count, head_width)
    key_heads = key_rows[0].reshape(block_size, head_count, head_width)
    value_heads = value_rows[0].reshape(block_size, head_count, head_width)
    within, rising, falling = decay_tables(decay_rates, block_size)
    step_decay = jnp.exp(-decay_rates * block_size)
    identity_pair = (
        jnp.ones((head_count,), jnp.float32),
        jnp.zeros((head_count, head_width, head_width), jnp.float32),
    )
    scaled_keys = (key_heads * falling[:, :, None]).astype(jnp.bfloat16)
    span_state = jnp.einsum(
        "shd,she->hde", scaled_keys, value_heads, preferred_element_type=jnp.float32
    )
    prefix = prefix_2((step_decay, span_state), "seq", combine_states, identity_pair, False)[1]
    scores = jnp.einsum("thd,shd->hts", query_heads, key_heads, preferred_element_type=jnp.float32)
    mixing = (scores * within).astype(jnp.bfloat16)
    prefix_half = prefix.astype(jnp.bfloat16)
    inner_part = jnp.einsum("hts,she->the", mixing, value_heads, preferred_element_type=jnp.float32)
    outer_part = rising[:, :, None] * jnp.einsum(
        "thd,hde->the", query_heads, prefix_half, preferred_element_type=jnp.float32
    )
    attended = inner_part + outer_part
    spread = jnp.sqrt(jnp.mean(attended * attended, axis=-1, keepdims=True) + norm_epsilon)
    normed = attended / spread
    gain_heads = norm_gain.reshape(head_count, head_width)
    probe_heads = reward_probe.reshape(head_count, head_width)
    weights = gain_heads * probe_heads
    logits = jnp.sum(normed * weights[None], axis=(1, 2))
    positions = lax.axis_index("seq") * block_size + jnp.arange(block_size)
    segment = jnp.sum((step_ends[0][None, :] < positions[:, None]).astype(jnp.int32), axis=1)
    picked = (segment[:, None] == jnp.arange(STEPS)[None, :]).astype(jnp.float32)
    fractions = step_counts[0].astype(jnp.float32) / ROLLOUTS
    targets = jnp.sum(picked * fractions[None, :], axis=1)
    token_loss = jax.nn.softplus(logits) - targets * logits
    loss_part = jnp.sum(token_loss) / length
    slope_term = loss_scaling * (jax.nn.sigmoid(logits) - targets) / length
    gain_part = jnp.sum(slope_term[:, None, None] * normed * probe_heads[None], axis=0).reshape(-1)
    probe_part = jnp.sum(slope_term[:, None, None] * normed * gain_heads[None], axis=0).reshape(-1)
    lifted = slope_term[:, None, None] * weights[None]
    out_grad = (
        (lifted - normed * jnp.mean(lifted * normed, axis=-1, keepdims=True)) / spread
    ).astype(jnp.bfloat16)
    scaled_queries = (query_heads * rising[:, :, None]).astype(jnp.bfloat16)
    partial_state = jnp.einsum(
        "thd,the->hde", scaled_queries, out_grad, preferred_element_type=jnp.float32
    )
    summed = lax.psum((loss_part, gain_part, probe_part), ("dp", "seq"))
    later = prefix_2((step_decay, partial_state), "seq", combine_states, identity_pair, True)[1]
    later_half = later.astype(jnp.bfloat16)
    back_scores = jnp.einsum(
        "the,she->hts", out_grad, value_heads, preferred_element_type=jnp.float32
    )
    back_mix = (back_scores * within).astype(jnp.bfloat16)
    grad_q = jnp.einsum("hts,shd->thd", back_mix, key_heads, preferred_element_type=jnp.float32)
    grad_q = grad_q + rising[:, :, None] * jnp.einsum(
        "the,hde->thd", out_grad, prefix_half, preferred_element_type=jnp.float32
    )
    grad_k = jnp.einsum("hts,thd->shd", back_mix, query_heads, preferred_element_type=jnp.float32)
    grad_k = grad_k + falling[:, :, None] * jnp.einsum(
        "she,hde->shd", value_heads, later_half, preferred_element_type=jnp.float32
    )
    grad_v = jnp.einsum("hts,the->she", mixing, out_grad, preferred_element_type=jnp.float32)
    grad_v = grad_v + falling[:, :, None] * jnp.einsum(
        "shd,hde->she", key_heads, later_half, preferred_element_type=jnp.float32
    )
    flat_shape = (1, block_size, head_count * head_width)
    return (
        summed[0],
        grad_q.astype(jnp.bfloat16).reshape(flat_shape),
        grad_k.astype(jnp.bfloat16).reshape(flat_shape),
        grad_v.astype(jnp.bfloat16).reshape(flat_shape),
        summed[1],
        summed[2],
    )


def solution(mesh):
    in_specs = (
        P("dp", "seq", None),
        P("dp", "seq", None),
        P("dp", "seq", None),
        P(),
        P(),
        P(),
        P("dp", None),
        P("dp", None),
    )
    out_specs = (P(), P("dp", "seq", None), P("dp", "seq", None), P("dp", "seq", None), P(), P())
    return jax.shard_map(
        on_device, mesh=mesh, in_specs=in_specs, out_specs=out_specs, check_vma=False
    )
```

profile of v0, /device:TPU:0, one launch (start us, length us, event | category | flops | bytes accessed | tf_op | source)
XLA Modules:
  0.0 522.0 jit_solution(13856354450567873825)
XLA Ops:
  7.2 0.0 all-gather.6.cloned.1.call-start
  7.2 0.0 copy-start.16
  7.2 1.7 copy.51
  8.9 0.0 copy-start.1
  9.0 0.0 copy-done.13
  9.0 0.2 copy.77
  9.2 0.0 copy-start
  9.2 0.1 multiply_exponential_fusion
  9.3 2.1 fusion.10
  11.4 0.0 copy-start.15
  11.4 0.0 all-gather.6.cloned.1.call-update
  11.4 0.0 all-gather.8.cloned.1.call-start
  11.5 0.6 copy-done.19
  12.0 0.6 dynamic-slice
  13.3 0.1 exponential_dynamic-update-slice_fusion
  13.4 23.6 %all-reduce = f32[256]{0:T(256)S(1)} all-reduce(f32[256]{0:T(256)S(1)} %get-tuple-element.184), channel_id=2, replica_groups=mesh['dp'=4,'seq'=8] {'seq'}, use_global_device_ids=true, to_apply=%add | all-reduce | flops 256 | bytes 2048
  37.0 0.1 reshape.208
  37.1 1.6 copy.50
  38.7 0.0 copy-done.17
  38.7 0.1 convert_reduce_fusion
  38.8 0.1 select_reduce_fusion
  38.9 0.1 subtract_compare_fusion
  39.0 0.1 subtract_select_fusion
  39.1 0.8 multiply_convert_fusion.3
  40.0 0.0 copy-done
  40.0 0.0 copy-start.11
  40.0 1.0 copy-done.11
  41.0 2.2 fusion.14
  43.2 198.9 %all-gather.6.cloned.1.call-done = f32[256,128,128]{2,1,0:T(8,128)} async-done(((f32[32,128,128]{2,1,0:T(8,128)}), f32[256,128,128]{2,1,0:T(8,128)}) %all-gather.6.cloned.1.call-update) | async-done | bytes 16777232 | tf_op jit(solution)/shard_map/all_gather | solution.py:18
  242.0 0.2 broadcast_in_dim.17.clone
  242.3 2.2 multiply_reduce_fusion.3
  244.5 0.7 multiply_reduce_fusion.2
  245.2 0.6 fusion.26
  245.9 3.1 multiply_reduce_fusion
  249.0 0.7 fusion.2
  249.7 0.0 copy-start.4
  249.7 1.0 copy-done.4
  250.7 2.1 fusion.11
  252.8 0.0 all-gather.8.cloned.1.call-update
  253.5 56.5 %all-reduce.1 = (f32[]{:T(128)}, f32[4096]{0:T(1024)}, f32[4096]{0:T(1024)}) all-reduce(f32[]{:T(128)S(6)} %div.47, f32[4096]{0:T(1024)S(1)} %bitcast.101, f32[4096]{0:T(1024)S(1)} %bitcast.100), channel_id=1, replica_groups=mesh['dp'=4,'seq'=8] {'dp','seq'}, use_global_device_ids=true, to_apply=%region_7.8 | all-reduce | flops 8193 | bytes 65544 | tf_op jit(solution)/shard_map/psum | solution.py:101
  310.0 2.7 multiply_convert_fusion.1
  312.6 0.0 copy-start.5
  312.7 0.8 fusion.28
  313.5 0.1 copy-done.8
  313.6 0.6 copy-done.5
  314.3 1.5 fusion.8
  315.7 2.4 copy.65
  318.2 1.8 fusion.29
  319.9 173.9 %all-gather.8.cloned.1.call-done = f32[256,128,128]{2,1,0:T(8,128)} async-done(((f32[32,128,128]{2,1,0:T(8,128)}), f32[256,128,128]{2,1,0:T(8,128)}) %all-gather.8.cloned.1.call-update) | async-done | bytes 16777232 | tf_op jit(solution)/shard_map/all_gather | solution.py:18
  493.8 0.2 broadcast_in_dim.17
  494.0 14.1 %while.27 = (s32[]{:T(128)}, f32[32,128,128]{2,1,0:T(8,128)S(1)}, s32[]{:T(128)}, f32[8,32]{1,0:T(8,128)S(1)}, f32[8,32,128,128]{3,2,1,0:T(8,128)}, /*index=5*/s32[]{:T(128)}, s32[]{:T(128)}, s32[]{:T(128)}, s32[]{:T(128)}) while((s32[]{:T(128)}, f32[32,128,128]{2,1,0:T(8,128)S(1)}, s32[]{:T(128)}, f32[8,32]{1,0:T(8,128)S(1)}, ...), condition=%wide.region_10.11_spmd, body=%wide.region_9.10_spmd.sunk | while | flops 1048582 | bytes 6291995 | solution.py:27
  494.1 2.0 bitcast_add_fusion.5
  496.1 2.0 bitcast_add_fusion.5
  498.1 2.0 bitcast_add_fusion.5
  500.1 2.0 bitcast_add_fusion.5
  502.1 2.0 bitcast_add_fusion.5
  504.2 2.0 bitcast_add_fusion.5
  506.2 2.0 bitcast_add_fusion.5
  508.2 2.2 fusion.16
  510.4 1.6 fusion.4
  512.0 0.5 fusion.6
  512.5 0.0 copy-start.10
  512.6 1.3 copy.66
  513.9 1.3 copy.67
  (40 shorter events, 0.2 us)
Async XLA Ops:
  7.2 1.8 copy-start.13
  7.2 234.9 %all-gather.6.cloned.1.call-start = ((), (), s32[]{:S(2)}) async-start(), calls=%async_computation | async-start | bytes 18874368 | tf_op jit(solution)/shard_map/all_gather | solution.py:18
  7.2 2.0 copy-start.16
  8.9 30.2 %copy-start.1 = (bf16[1,128,4096]{1,2,0:T(8,128)(2,1)}, bf16[1,128,4096]{1,2,0:T(8,128)(2,1)S(1)}, u32[]{:S(2)}) copy-start(bf16[1,128,4096]{1,2,0:T(8,128)(2,1)S(1)} %copy.51) | copy-start | bytes 3145732
  9.2 30.8 %copy-start = (bf16[16,8,32,128]{3,2,1,0:T(8,128)(2,1)}, bf16[16,8,32,128]{3,2,1,0:T(8,128)(2,1)S(1)}, u32[]{:S(2)}) copy-start(bf16[16,8,32,128]{3,2,1,0:T(8,128)(2,1)S(1)} %copy.77) | copy-start | bytes 3145732
  11.4 0.7 copy-start.19
  11.4 27.3 %copy-start.17 = (s32[1,64]{1,0:T(1,128)S(1)}, s32[1,64]{1,0:T(1,128)}, u32[]{:S(2)}) copy-start(s32[1,64]{1,0:T(1,128)} %param.18) | copy-start | bytes 772
  11.4 27.4 %copy-start.18 = (s32[1,64]{1,0:T(1,128)S(1)}, s32[1,64]{1,0:T(1,128)}, u32[]{:S(2)}) copy-start(s32[1,64]{1,0:T(1,128)} %param.19) | copy-start | bytes 772
  11.4 27.6 %copy-start.14 = (f32[4096]{0:T(1024)S(1)}, f32[4096]{0:T(1024)}, u32[]{:S(2)}) copy-start(f32[4096]{0:T(1024)} %param.17) | copy-start | bytes 49156
  11.4 27.6 %copy-start.15 = (f32[4096]{0:T(1024)S(1)}, f32[4096]{0:T(1024)}, u32[]{:S(2)}) copy-start(f32[4096]{0:T(1024)} %param.16) | copy-start | bytes 49156
  11.4 482.4 %all-gather.8.cloned.1.call-start = ((), (), s32[]{:S(2)}) async-start(), calls=%async_computation.1 | async-start | bytes 18874368 | tf_op jit(solution)/shard_map/all_gather | solution.py:18
  40.0 1.0 copy-start.11
  249.7 1.0 copy-start.4
  310.0 2.7 copy-start.2
  312.6 1.0 copy-start.8
  312.6 1.6 copy-start.5
  315.7 2.4 copy-start.6
  315.7 2.4 copy-start.12
  508.2 2.3 copy-start.3
  508.2 2.3 copy-start.7
  510.4 1.6 copy-start.9
  512.5 1.3 copy-start.10
Sparse Core Ops, SparseCore 0:
  11.5 230.4 all-gather.5
  253.0 240.7 all-gather.7
where the time goes:
time: 523 us; the launch traced here: 522 us
  waiting for transfers between devices  373 us (71%)
  blocking collectives  80.1 us (15%)
  matrix products  20.5 us (4%)
  other arithmetic  19.6 us (4%)
  between operations  15.7 us (3%)
  local copies, waits for them, and re-layouts  13.1 us (3%)
    all_gather x2, waiting for transfers between devices, prefix_2(): gathered = jax.tree.map(lambda a: lax.all_gather(a, axis), part)  373 us
    psum x1, blocking collectives, on_device(): summed = lax.psum((loss_part, gain_part, probe_part), ('dp', 'seq'))  56.5 us
    unnamed x1, blocking collectives  23.6 us
    add x7, other arithmetic, combine_states(): second_part[0][:, None, None] * first_part[1] + second_part[1]  13.8 us
    unnamed x48, local copies, waits for them, and re-layouts  12.5 us
  transfers between devices with their start and end apart: 2, of which 2 were waited for; matrix products, arithmetic and copies ran while one was open for 3% of the time, Pallas kernels for 0%

commit v1 on v0

v1 whole, which is shorter than its diff:
```python
import functools

import jax
import jax.numpy as jnp
from jax import lax
from jax.experimental import pallas as pl
from jax.experimental.pallas import tpu as pltpu
from jax.sharding import PartitionSpec as P

ROLLOUTS = 8
CHUNK = 2
loss_scaling = 32768.0
norm_epsilon = 1e-06
MESH = pl.DeviceIdType.MESH
F32 = jnp.float32
BF16 = jnp.bfloat16


def dot(a, b, ca, cb):
    return lax.dot_general(a, b, (((ca,), (cb,)), ((), ())), preferred_element_type=F32)


def bits_of(count):
    steps = []
    bit = 1
    while bit < count:
        steps.append(bit)
        bit *= 2
    return steps


def layer(
    n_dp,
    n_seq,
    rates_ref,
    q_ref,
    k_ref,
    v_ref,
    gain_ref,
    probe_ref,
    ends_ref,
    counts_ref,
    loss_ref,
    gq_ref,
    gk_ref,
    gv_ref,
    ggain_ref,
    gprobe_ref,
    state,
    peer,
    cin,
    cout,
    give,
    take,
    bstate,
    bpeer,
    bcin,
    bcout,
    bgive,
    btake,
    prefix_half,
    mix,
    normed,
    slim,
    gk_part,
    gv_part,
    og,
    sq,
    logit_sum,
    sums,
    sums_in,
    send_a,
    recv_a,
    send_c,
    recv_c,
    send_p,
    recv_p,
    bsend_a,
    brecv_a,
    bsend_c,
    brecv_c,
    bsend_p,
    brecv_p,
    send_s,
    recv_s,
):
    heads = rates_ref.shape[0]
    span = q_ref.shape[0]
    width = q_ref.shape[1] // heads
    half = heads // 2
    chunks = half // CHUNK
    length = span * n_seq
    seq = lax.axis_index("seq")
    dp = lax.axis_index("dp")
    column = seq % 2
    group = seq // 2
    groups = n_seq // 2
    mate = seq + 1 - 2 * column
    own = column * half
    other = (1 - column) * half

    exchanges = []
    for bit in bits_of(n_dp):
        exchanges.append(("dp", dp + bit * (1 - 2 * ((dp // bit) % 2))))
    for bit in bits_of(n_seq):
        exchanges.append(("seq", seq + bit * (1 - 2 * ((seq // bit) % 2))))

    barrier = pltpu.get_barrier_semaphore()
    for axis, partner in exchanges:
        pl.semaphore_signal(barrier, inc=1, device_id={axis: partner}, device_id_type=MESH)

    @pl.when(group > 0)
    def _():
        pl.semaphore_signal(barrier, inc=1, device_id={"seq": seq - 2}, device_id_type=MESH)

    @pl.when(group < groups - 1)
    def _():
        pl.semaphore_signal(barrier, inc=1, device_id={"seq": seq + 2}, device_id_type=MESH)

    @pl.when(group == 0)
    def _():
        cin[...] = jnp.zeros_like(cin)

    @pl.when(group == groups - 1)
    def _():
        bcin[...] = jnp.zeros_like(bcin)

    logit_sum[...] = jnp.zeros_like(logit_sum)

    rows = lax.broadcasted_iota(jnp.int32, (span, width), 0).astype(F32)
    gap = (
        lax.broadcasted_iota(jnp.int32, (span, span), 0)
        - lax.broadcasted_iota(jnp.int32, (span, span), 1)
    ).astype(F32)
    causal = gap >= 0.0

    def cols(h):
        return pl.ds(pl.multiple_of(h * width, width), width)

    def within_of(h):
        return jnp.where(causal, jnp.exp(-rates_ref[h] * jnp.where(causal, gap, 0.0)), 0.0)

    def rising_of(h):
        return jnp.exp(-rates_ref[h] * rows)

    def falling_of(h):
        return jnp.exp(-rates_ref[h] * (span - rows))

    def copy(src, dst, send, recv, at, rel, j, target):
        return pltpu.make_async_remote_copy(
            src_ref=src.at[pl.ds(at, CHUNK)],
            dst_ref=dst.at[pl.ds(rel, CHUNK)],
            send_sem=send.at[j],
            recv_sem=recv.at[j],
            device_id={"seq": target},
            device_id_type=MESH,
        )

    def swap(j, back):
        if back:
            return copy(bstate, bpeer, bsend_a, brecv_a, other + j * CHUNK, j * CHUNK, j, mate)
        return copy(state, peer, send_a, recv_a, other + j * CHUNK, j * CHUNK, j, mate)

    def hop(j, back):
        if back:
            return copy(bcout, bcin, bsend_c, brecv_c, j * CHUNK, j * CHUNK, j, seq - 2)
        return copy(cout, cin, send_c, recv_c, j * CHUNK, j * CHUNK, j, seq + 2)

    def hand(j, back):
        if back:
            return copy(bgive, btake, bsend_p, brecv_p, j * CHUNK, j * CHUNK, j, mate)
        return copy(give, take, send_p, recv_p, j * CHUNK, j * CHUNK, j, mate)

    def chain(j, back):
        mine_ref, peer_ref, in_ref, out_ref, give_ref = (
            (bstate, bpeer, bcin, bcout, bgive) if back else (state, peer, cin, cout, give)
        )
        leads = (column == 1) if back else (column == 0)
        has_in = (group < groups - 1) if back else (group > 0)
        has_out = (group > 0) if back else (group < groups - 1)
        swap(j, back).wait_recv()

        @pl.when(has_in)
        def _():
            hop(j, back).wait_recv()

        kept = []
        for i in range(CHUNK):
            rel = j * CHUNK + i
            h = own + rel
            decay = jnp.exp(jnp.full((1, width), -rates_ref[h] * span, F32))
            one = jnp.ones_like(decay)
            zero = jnp.zeros_like(decay)
            lead_decay = jnp.where(leads, decay, one)
            trail_decay = jnp.where(leads, one, decay)
            mine = mine_ref[h]
            theirs = peer_ref[rel]
            carry = in_ref[rel]
            out_ref[rel] = decay * decay * carry + lead_decay * mine + trail_decay * theirs
            give_ref[rel] = lead_decay * carry + jnp.where(leads, one, zero) * mine
            kept.append(
                (trail_decay * carry + jnp.where(leads, zero, one) * theirs).astype(BF16)
            )

        @pl.when(has_out)
        def _():
            hop(j, back).start()

        hand(j, back).start()
        return kept

    def make_state(h):
        keys = (k_ref[:, cols(h)].astype(F32) * falling_of(h)).astype(BF16)
        state[h] = dot(keys, v_ref[:, cols(h)], 0, 0)

    def finish_front(h, inner, prefix):
        prefix_half[h] = prefix
        q = q_ref[:, cols(h)]
        attended = inner + rising_of(h) * dot(q, prefix, 1, 0)
        inverse = lax.rsqrt(jnp.mean(attended * attended, axis=1, keepdims=True) + norm_epsilon)
        unit = attended * inverse
        normed[h] = unit
        weights = gain_ref[pl.ds(h, 1), :] * probe_ref[pl.ds(h, 1), :]
        weighted = unit * weights
        slim[h] = (weights - unit * jnp.mean(weighted, axis=1, keepdims=True)) * inverse
        logit_sum[...] += weighted

    def inner_of(h):
        q = q_ref[:, cols(h)]
        mixed = (dot(q, k_ref[:, cols(h)], 1, 1) * within_of(h)).astype(BF16)
        mix[h] = mixed
        sq[h] = (q.astype(F32) * rising_of(h)).astype(BF16)
        return dot(mixed, v_ref[:, cols(h)], 1, 0)

    def make_first(j, carry):
        for i in range(CHUNK):
            make_state(other + j * CHUNK + i)
        return carry

    make_first(0, 0)
    edges = jnp.where(group > 0, 1, 0) + jnp.where(group < groups - 1, 1, 0)
    pl.semaphore_wait(barrier, len(exchanges) + edges)
    swap(0, False).start()

    def send_first(j, carry):
        make_first(j, carry)
        swap(j, False).start()
        return carry

    lax.fori_loop(1, chunks, send_first, 0)

    def forward(j, carry):
        for i in range(CHUNK):
            make_state(own + j * CHUNK + i)
        kept = chain(j, False)
        for i in range(CHUNK):
            h = own + j * CHUNK + i
            finish_front(h, inner_of(h), kept[i])
            h = other + j * CHUNK + i
            gk_part[h] = inner_of(h)
        return carry

    lax.fori_loop(0, chunks, forward, 0)

    def forward_rest(j, carry):
        hand(j, False).wait_recv()
        for i in range(CHUNK):
            rel = j * CHUNK + i
            h = other + rel
            finish_front(h, gk_part[h], take[rel].astype(BF16))
        return carry

    lax.fori_loop(0, chunks, forward_rest, 0)

    steps = ends_ref.shape[1]
    position = seq * span + lax.broadcasted_iota(jnp.int32, (span, steps), 0)
    segment = jnp.sum(jnp.where(ends_ref[...] < position, 1.0, 0.0), axis=1, keepdims=True)
    step_at = lax.broadcasted_iota(jnp.int32, (span, steps), 1).astype(F32)
    fractions = counts_ref[...].astype(F32) / ROLLOUTS
    targets = jnp.sum(jnp.where(step_at == segment, fractions, 0.0), axis=1, keepdims=True)
    logits = jnp.sum(logit_sum[...], axis=1, keepdims=True)
    soft = jnp.maximum(logits, 0.0) + jnp.log1p(jnp.exp(-jnp.abs(logits)))
    loss = jnp.sum(soft - targets * logits, axis=0, keepdims=True) / length
    slope = loss_scaling * (jax.nn.sigmoid(logits) - targets) / length
    slope_wide = jnp.broadcast_to(slope, (span, width))
    logit_sum[...] = slope_wide
    sums[0, pl.ds(heads, 8), :] = jnp.broadcast_to(loss, (8, width))

    def make_back(h):
        steep = logit_sum[...]
        grad = (steep * slim[h]).astype(BF16)
        og[h] = grad
        bstate[h] = dot(sq[h], grad, 0, 0)
        sums[0, pl.ds(h, 1), :] = jnp.sum(steep * normed[h], axis=0, keepdims=True)

    def send_back(j, carry):
        for i in range(CHUNK):
            make_back(other + j * CHUNK + i)
        swap(j, True).start()
        return carry

    lax.fori_loop(0, chunks, send_back, 0)

    def back_parts(h):
        grad = og[h]
        k = k_ref[:, cols(h)]
        q = q_ref[:, cols(h)]
        back_mix = (dot(grad, v_ref[:, cols(h)], 1, 1) * within_of(h)).astype(BF16)
        grad_q = dot(back_mix, k, 1, 0) + rising_of(h) * dot(grad, prefix_half[h], 1, 1)
        gq_ref[:, cols(h)] = grad_q.astype(BF16)
        return dot(back_mix, q, 0, 0), dot(mix[h], grad, 0, 0)

    def finish_back(h, grad_k, grad_v, later):
        falling = falling_of(h)
        grad_k = grad_k + falling * dot(v_ref[:, cols(h)], later, 1, 1)
        grad_v = grad_v + falling * dot(k_ref[:, cols(h)], later, 1, 0)
        gk_ref[:, cols(h)] = grad_k.astype(BF16)
        gv_ref[:, cols(h)] = grad_v.astype(BF16)

    def backward(j, carry):
        for i in range(CHUNK):
            make_back(own + j * CHUNK + i)
        kept = chain(j, True)
        for i in range(CHUNK):
            h = own + j * CHUNK + i
            grad_k, grad_v = back_parts(h)
            finish_back(h, grad_k, grad_v, kept[i])
            h = other + j * CHUNK + i
            gk_part[h], gv_part[h] = back_parts(h)
        return carry

    lax.fori_loop(0, chunks, backward, 0)

    def total(at):
        axis, partner = exchanges[at]
        return pltpu.make_async_remote_copy(
            src_ref=sums.at[at],
            dst_ref=sums_in.at[at],
            send_sem=send_s.at[at],
            recv_sem=recv_s.at[at],
            device_id={axis: partner},
            device_id_type=MESH,
        )

    def backward_rest(j):
        hand(j, True).wait_recv()
        for i in range(CHUNK):
            rel = j * CHUNK + i
            h = other + rel
            finish_back(h, gk_part[h], gv_part[h], btake[rel].astype(BF16))

    total(0).start()
    for j in range(max(chunks, len(exchanges))):
        if j < chunks:
            backward_rest(j)
        if j < len(exchanges):
            total(j).wait_recv()
            sums[j + 1] = sums[j] + sums_in[j]
            if j + 1 < len(exchanges):
                total(j + 1).start()

    last = len(exchanges)
    summed = sums[last, pl.ds(0, heads), :]
    ggain_ref[...] = summed * probe_ref[...]
    gprobe_ref[...] = summed * gain_ref[...]
    loss_ref[...] = sums[last, pl.ds(heads, 1), pl.ds(0, 1)]

    for at in range(len(exchanges)):
        total(at).wait_send()

    def drain(j, carry):
        for back in (False, True):
            swap(j, back).wait_send()
            hand(j, back).wait_send()

        @pl.when(group < groups - 1)
        def _():
            hop(j, False).wait_send()

        @pl.when(group > 0)
        def _():
            hop(j, True).wait_send()

        return carry

    lax.fori_loop(0, chunks, drain, 0)


def solution(mesh):
    n_dp = mesh.shape["dp"]
    n_seq = mesh.shape["seq"]
    exchanges = len(bits_of(n_dp)) + len(bits_of(n_seq))

    def on_device(
        queries, key_rows, value_rows, decay_rates, norm_gain, reward_probe, step_ends, step_counts
    ):
        heads = decay_rates.shape[0]
        _, span, features = queries.shape
        width = features // heads
        half = heads // 2
        chunks = half // CHUNK
        vmem = pl.BlockSpec(memory_space=pltpu.VMEM)
        rows = jax.ShapeDtypeStruct((span, features), BF16)
        table = jax.ShapeDtypeStruct((heads, width), F32)

        def scan_buffers():
            return [pltpu.VMEM((heads, width, width), F32)] + [
                pltpu.VMEM((half, width, width), F32)
            ] * 5

        loss, gq, gk, gv, ggain, gprobe = pl.pallas_call(
            functools.partial(layer, n_dp, n_seq),
            out_shape=(jax.ShapeDtypeStruct((1, 1), F32), rows, rows, rows, table, table),
            in_specs=[pl.BlockSpec(memory_space=pltpu.SMEM)] + [vmem] * 7,
            out_specs=(vmem,) * 6,
            scratch_shapes=scan_buffers()
            + scan_buffers()
            + [
                pltpu.VMEM((heads, width, width), BF16),
                pltpu.VMEM((heads, span, span), BF16),
                pltpu.VMEM((heads, span, width), F32),
                pltpu.VMEM((heads, span, width), F32),
                pltpu.VMEM((heads, span, width), F32),
                pltpu.VMEM((heads, span, width), F32),
                pltpu.VMEM((heads, span, width), BF16),
                pltpu.VMEM((heads, span, width), BF16),
                pltpu.VMEM((span, width), F32),
                pltpu.VMEM((exchanges + 1, heads + 8, width), F32),
                pltpu.VMEM((exchanges, heads + 8, width), F32),
            ]
            + [pltpu.SemaphoreType.DMA((chunks,))] * 12
            + [pltpu.SemaphoreType.DMA((exchanges,))] * 2,
            compiler_params=pltpu.CompilerParams(
                collective_id=0, has_side_effects=True, vmem_limit_bytes=48 * 1024 * 1024
            ),
            cost_estimate=pl.CostEstimate(
                flops=28 * heads * span * width * width,
                bytes_accessed=12 * span * features,
                transcendentals=6 * heads * span * width,
            ),
        )(
            decay_rates,
            queries[0],
            key_rows[0],
            value_rows[0],
            norm_gain.reshape(heads, width),
            reward_probe.reshape(heads, width),
            step_ends,
            step_counts,
        )
        return (
            loss.reshape(()),
            gq[None],
            gk[None],
            gv[None],
            ggain.reshape(features),
            gprobe.reshape(features),
        )

    rows = P("dp", "seq", None)
    return jax.shard_map(
        on_device,
        mesh=mesh,
        in_specs=(rows, rows, rows, P(), P(), P(), P("dp", None), P("dp", None)),
        out_specs=(P(), rows, rows, rows, P(), P()),
        check_vma=False,
    )
```

time: 523 us -> 119 us (0.23)
  waiting for transfers between devices: 373 us -> 0 us
  Pallas kernels: 0 us -> 108 us
  blocking collectives: 80.1 us -> 0 us
  matrix products: 20.5 us -> 0 us
  other arithmetic: 19.6 us -> 0 us
  between operations: 15.7 us -> 2.36 us
    all_gather x2 -> x0, waiting for transfers between devices: 373 us -> none  [prefix_2(): gathered = jax.tree.map(lambda a: lax.all_gather(a, axis), part)]
    pallas_call x0 -> x1, Pallas kernels: none -> 108 us  [on_device(): pl.pallas_call(functools.partial(layer, n_dp, n_seq), out_shape=(jax.Shap...]
    psum x1 -> x0, blocking collectives: 56.5 us -> none  [on_device(): summed = lax.psum((loss_part, gain_part, probe_part), ('dp', 'seq'))]
    unnamed x1 -> x0, blocking collectives: 23.6 us -> none
    dot_general x12 -> x0, matrix products: 20.5 us -> none  [the longest x1 2.66 us: on_device(): jnp.einsum('the,she->hts', out_grad, value_heads, preferred_element_type=...]
    add x8 -> x0, other arithmetic: 13.8 us -> none  [the longest x7 13.8 us: combine_states(): second_part[0][:, None, None] * first_part[1] + second_part[1]]
    unnamed x48 -> x19, local copies, waits for them, and re-layouts: 12.5 us -> 8.67 us
  transfers between devices with their start and end apart: 2 -> 0, of which waited for: 2 -> 0; matrix products, arithmetic and copies ran while one was open for 3% -> 0% of each run, Pallas kernels for 0% -> 0%
where the time goes in v1:
time: 119 us
  Pallas kernels  108 us (91%)
  local copies, waits for them, and re-layouts  8.67 us (7%)
  between operations  2.36 us (2%)
    pallas_call x1, Pallas kernels, on_device(): pl.pallas_call(functools.partial(layer, n_dp, n_seq), out_shape=(jax.Shap...  108 us
    unnamed x19, local copies, waits for them, and re-layouts  8.67 us

profile of v1, /device:TPU:0, one launch (start us, length us, event | category | flops | bytes accessed | tf_op | source)
XLA Modules:
  0.0 118.6 jit_solution(8945857614695058536)
XLA Ops:
  0.6 0.0 copy-start.4
  0.6 0.0 copy-start.5
  0.7 0.0 copy-start.6
  0.7 0.6 copy-done.4
  1.3 0.0 copy-done.5
  1.3 0.0 copy-done.6
  1.3 0.0 copy-start
  1.3 1.2 %copy-done = bf16[1,128,4096]{2,1,0:T(8,128)(2,1)S(1)} copy-done((bf16[1,128,4096]{2,1,0:T(8,128)(2,1)S(1)}, bf16[1,128,4096]{2,1,0:T(8,128)(2,1)}, u32[]{:S(2)}) %copy-start) | copy-done | bytes 1048600
  2.5 0.0 copy-start.1
  2.5 1.2 %copy-done.1 = bf16[1,128,4096]{2,1,0:T(8,128)(2,1)S(1)} copy-done((bf16[1,128,4096]{2,1,0:T(8,128)(2,1)S(1)}, bf16[1,128,4096]{2,1,0:T(8,128)(2,1)}, u32[]{:S(2)}) %copy-start.1) | copy-done | bytes 1048600
  3.8 0.0 copy-start.2
  3.8 0.7 copy-done.2
  4.5 0.0 copy-start.3
  4.5 0.7 copy-done.3
  5.2 107.6 %shard_map.127 = (f32[1,1]{1,0:T(1,128)}, bf16[128,4096]{1,0:T(8,128)(2,1)S(1)}, bf16[128,4096]{1,0:T(8,128)(2,1)S(1)}, bf16[128,4096]{1,0:T(8,128)(2,1)S(1)}, f...) custom-call(f32[32]{0:T(128)S(1)} %copy-done.4, bf16[128,4096]{1,0:T(8,128)(2,1)S(1)} %bitcast.16, ...), custom_call_target="tpu_custom_call" | custom-call | flops 1879048192 | bytes 6291456 | tf_op jit(solution)/shard_map/pallas_call | solution.py:411
  113.3 1.0 copy.21
  114.3 1.0 copy.22
  115.3 1.0 copy.23
  116.2 0.6 copy.24
  116.9 0.6 copy.25
Async XLA Ops:
  0.6 0.7 copy-start.4
  0.6 0.7 copy-start.5
  0.7 0.7 copy-start.6
  1.3 1.2 %copy-start = (bf16[1,128,4096]{2,1,0:T(8,128)(2,1)S(1)}, bf16[1,128,4096]{2,1,0:T(8,128)(2,1)}, u32[]{:S(2)}) copy-start(bf16[1,128,4096]{2,1,0:T(8,128)(2,1)} %param.8) | copy-start | bytes 3145732
  2.5 1.2 %copy-start.1 = (bf16[1,128,4096]{2,1,0:T(8,128)(2,1)S(1)}, bf16[1,128,4096]{2,1,0:T(8,128)(2,1)}, u32[]{:S(2)}) copy-start(bf16[1,128,4096]{2,1,0:T(8,128)(2,1)} %param.9) | copy-start | bytes 3145732
  3.8 0.7 copy-start.2
  4.5 0.7 copy-start.3

commit v2 on v1

--- a/solution.py
+++ b/solution.py
@@ -9,6 +9,7 @@
 
 ROLLOUTS = 8
 CHUNK = 2
+FLIGHT = 2
 loss_scaling = 32768.0
 norm_epsilon = 1e-06
 MESH = pl.DeviceIdType.MESH
@@ -59,6 +60,7 @@
     bgive,
     btake,
     prefix_half,
+    later_half,
     mix,
     normed,
     slim,
@@ -178,13 +180,11 @@
         leads = (column == 1) if back else (column == 0)
         has_in = (group < groups - 1) if back else (group > 0)
         has_out = (group > 0) if back else (group < groups - 1)
-        swap(j, back).wait_recv()
 
         @pl.when(has_in)
         def _():
             hop(j, back).wait_recv()
 
-        kept = []
         for i in range(CHUNK):
             rel = j * CHUNK + i
             h = own + rel
@@ -198,23 +198,21 @@
             carry = in_ref[rel]
             out_ref[rel] = decay * decay * carry + lead_decay * mine + trail_decay * theirs
             give_ref[rel] = lead_decay * carry + jnp.where(leads, one, zero) * mine
-            kept.append(
-                (trail_decay * carry + jnp.where(leads, zero, one) * theirs).astype(BF16)
-            )
+            kept = (trail_decay * carry + jnp.where(leads, zero, one) * theirs).astype(BF16)
+            if back:
+                later_half[rel] = kept
+            else:
+                prefix_half[h] = kept
 
         @pl.when(has_out)
         def _():
             hop(j, back).start()
-
-        hand(j, back).start()
-        return kept
 
     def make_state(h):
         keys = (k_ref[:, cols(h)].astype(F32) * falling_of(h)).astype(BF16)
         state[h] = dot(keys, v_ref[:, cols(h)], 0, 0)
 
     def finish_front(h, inner, prefix):
-        prefix_half[h] = prefix
         q = q_ref[:, cols(h)]
         attended = inner + rising_of(h) * dot(q, prefix, 1, 0)
         inverse = lax.rsqrt(jnp.mean(attended * attended, axis=1, keepdims=True) + norm_epsilon)
@@ -237,40 +235,25 @@
             make_state(other + j * CHUNK + i)
         return carry
 
+    flight = min(FLIGHT, chunks)
+
+    def lead_first(j, carry):
+        make_first(j, carry)
+        swap(j, False).start()
+        return carry
+
     make_first(0, 0)
     edges = jnp.where(group > 0, 1, 0) + jnp.where(group < groups - 1, 1, 0)
     pl.semaphore_wait(barrier, len(exchanges) + edges)
     swap(0, False).start()
-
-    def send_first(j, carry):
-        make_first(j, carry)
-        swap(j, False).start()
-        return carry
-
-    lax.fori_loop(1, chunks, send_first, 0)
-
-    def forward(j, carry):
+    lax.fori_loop(1, flight, lead_first, 0)
+    lax.fori_loop(flight, chunks, make_first, 0)
+
+    def make_own(j):
         for i in range(CHUNK):
             make_state(own + j * CHUNK + i)
-        kept = chain(j, False)
-        for i in range(CHUNK):
-            h = own + j * CHUNK + i
-            finish_front(h, inner_of(h), kept[i])
-            h = other + j * CHUNK + i
-            gk_part[h] = inner_of(h)
-        return carry
-
-    lax.fori_loop(0, chunks, forward, 0)
-
-    def forward_rest(j, carry):
-        hand(j, False).wait_recv()
-        for i in range(CHUNK):
-            rel = j * CHUNK + i
-            h = other + rel
-            finish_front(h, gk_part[h], take[rel].astype(BF16))
-        return carry
-
-    lax.fori_loop(0, chunks, forward_rest, 0)
+
+    make_own(0)
 
     steps = ends_ref.shape[1]
     position = seq * span + lax.broadcasted_iota(jnp.int32, (span, steps), 0)
@@ -278,6 +261,59 @@
     step_at = lax.broadcasted_iota(jnp.int32, (span, steps), 1).astype(F32)
     fractions = counts_ref[...].astype(F32) / ROLLOUTS
     targets = jnp.sum(jnp.where(step_at == segment, fractions, 0.0), axis=1, keepdims=True)
+
+    def pace(i, back, after):
+        place = (groups - 1 - group) if back else group
+        at = i - jnp.minimum(2 * place, chunks - flight)
+
+        @pl.when((at >= 0) & (at < chunks))
+        def _():
+            chain(at, back)
+
+        @pl.when(i + flight < chunks)
+        def _():
+            swap(i + flight, back).start()
+
+        @pl.when((i + flight >= chunks) & (i + flight < 2 * chunks))
+        def _():
+            hand(i + flight - chunks, back).start()
+
+        @pl.when((at >= 0) & (at < chunks))
+        def _():
+            after(at)
+
+    def own_front(j):
+        for i in range(CHUNK):
+            h = own + j * CHUNK + i
+            finish_front(h, inner_of(h), prefix_half[h])
+
+    def forward(i, carry):
+        swap(i, False).wait_recv()
+        pace(i, False, own_front)
+
+        @pl.when(i + 1 < chunks)
+        def _():
+            make_own(i + 1)
+
+        for c in range(CHUNK):
+            h = other + i * CHUNK + c
+            gk_part[h] = inner_of(h)
+        return carry
+
+    lax.fori_loop(0, chunks, forward, 0)
+
+    def forward_rest(j, carry):
+        hand(j, False).wait_recv()
+        pace(j + chunks, False, own_front)
+        for i in range(CHUNK):
+            rel = j * CHUNK + i
+            h = other + rel
+            prefix_half[h] = take[rel].astype(BF16)
+            finish_front(h, gk_part[h], prefix_half[h])
+        return carry
+
+    lax.fori_loop(0, chunks, forward_rest, 0)
+
     logits = jnp.sum(logit_sum[...], axis=1, keepdims=True)
     soft = jnp.maximum(logits, 0.0) + jnp.log1p(jnp.exp(-jnp.abs(logits)))
     loss = jnp.sum(soft - targets * logits, axis=0, keepdims=True) / length
@@ -293,13 +329,24 @@
         bstate[h] = dot(sq[h], grad, 0, 0)
         sums[0, pl.ds(h, 1), :] = jnp.sum(steep * normed[h], axis=0, keepdims=True)
 
-    def send_back(j, carry):
+    def back_first(j, carry):
         for i in range(CHUNK):
             make_back(other + j * CHUNK + i)
+        return carry
+
+    def lead_back(j, carry):
+        back_first(j, carry)
         swap(j, True).start()
         return carry
 
-    lax.fori_loop(0, chunks, send_back, 0)
+    lax.fori_loop(0, flight, lead_back, 0)
+    lax.fori_loop(flight, chunks, back_first, 0)
+
+    def back_own(j):
+        for i in range(CHUNK):
+            make_back(own + j * CHUNK + i)
+
+    back_own(0)
 
     def back_parts(h):
         grad = og[h]
@@ -317,15 +364,22 @@
         gk_ref[:, cols(h)] = grad_k.astype(BF16)
         gv_ref[:, cols(h)] = grad_v.astype(BF16)
 
-    def backward(j, carry):
-        for i in range(CHUNK):
-            make_back(own + j * CHUNK + i)
-        kept = chain(j, True)
+    def own_back(j):
         for i in range(CHUNK):
             h = own + j * CHUNK + i
             grad_k, grad_v = back_parts(h)
-            finish_back(h, grad_k, grad_v, kept[i])
-            h = other + j * CHUNK + i
+            finish_back(h, grad_k, grad_v, later_half[j * CHUNK + i])
+
+    def backward(i, carry):
+        swap(i, True).wait_recv()
+        pace(i, True, own_back)
+
+        @pl.when(i + 1 < chunks)
+        def _():
+            back_own(i + 1)
+
+        for c in range(CHUNK):
+            h = other + i * CHUNK + c
             gk_part[h], gv_part[h] = back_parts(h)
         return carry
 
@@ -344,6 +398,7 @@
 
     def backward_rest(j):
         hand(j, True).wait_recv()
+        pace(j + chunks, True, own_back)
         for i in range(CHUNK):
             rel = j * CHUNK + i
             h = other + rel
@@ -417,6 +472,7 @@
             + scan_buffers()
             + [
                 pltpu.VMEM((heads, width, width), BF16),
+                pltpu.VMEM((half, width, width), BF16),
                 pltpu.VMEM((heads, span, span), BF16),
                 pltpu.VMEM((heads, span, width), F32),
                 pltpu.VMEM((heads, span, width), F32),

time: 119 us -> 114 us (0.958)
  Pallas kernels: 108 us -> 102 us
    pallas_call x1, Pallas kernels: 108 us -> 102 us  [on_device(): pl.pallas_call(functools.partial(layer, n_dp, n_seq), out_shape=(jax.Shap...]
where the time goes in v2:
time: 114 us; the launch traced here: 113 us
  Pallas kernels  102 us (89%)
  local copies, waits for them, and re-layouts  8.67 us (8%)
  between operations  2.36 us (2%)
    pallas_call x1, Pallas kernels, on_device(): pl.pallas_call(functools.partial(layer, n_dp, n_seq), out_shape=(jax.Shap...  102 us
    unnamed x19, local copies, waits for them, and re-layouts  8.67 us

profile of v2, /device:TPU:0, one launch (start us, length us, event | category | flops | bytes accessed | tf_op | source)
XLA Modules:
  0.0 113.2 jit_solution(12119788678502018851)
XLA Ops:
  0.6 0.0 copy-start.4
  0.6 0.0 copy-start.5
  0.7 0.0 copy-start.6
  0.7 0.6 copy-done.4
  1.3 0.0 copy-done.5
  1.3 0.0 copy-done.6
  1.3 0.0 copy-start
  1.3 1.2 %copy-done = bf16[1,128,4096]{2,1,0:T(8,128)(2,1)S(1)} copy-done((bf16[1,128,4096]{2,1,0:T(8,128)(2,1)S(1)}, bf16[1,128,4096]{2,1,0:T(8,128)(2,1)}, u32[]{:S(2)}) %copy-start) | copy-done | bytes 1048600
  2.5 0.0 copy-start.1
  2.5 1.2 %copy-done.1 = bf16[1,128,4096]{2,1,0:T(8,128)(2,1)S(1)} copy-done((bf16[1,128,4096]{2,1,0:T(8,128)(2,1)S(1)}, bf16[1,128,4096]{2,1,0:T(8,128)(2,1)}, u32[]{:S(2)}) %copy-start.1) | copy-done | bytes 1048600
  3.8 0.0 copy-start.2
  3.8 0.7 copy-done.2
  4.5 0.0 copy-start.3
  4.5 0.7 copy-done.3
  5.2 102.2 %shard_map.127 = (f32[1,1]{1,0:T(1,128)}, bf16[128,4096]{1,0:T(8,128)(2,1)S(1)}, bf16[128,4096]{1,0:T(8,128)(2,1)S(1)}, bf16[128,4096]{1,0:T(8,128)(2,1)S(1)}, f...) custom-call(f32[32]{0:T(128)S(1)} %copy-done.4, bf16[128,4096]{1,0:T(8,128)(2,1)S(1)} %bitcast.16, ...), custom_call_target="tpu_custom_call" | custom-call | flops 1879048192 | bytes 6291456 | tf_op jit(solution)/shard_map/pallas_call | solution.py:466
  108.0 1.0 copy.21
  108.9 1.0 copy.22
  109.9 1.0 copy.23
  110.9 0.6 copy.24
  111.5 0.6 copy.25
Async XLA Ops:
  0.6 0.7 copy-start.4
  0.6 0.7 copy-start.5
  0.7 0.7 copy-start.6
  1.3 1.2 %copy-start = (bf16[1,128,4096]{2,1,0:T(8,128)(2,1)S(1)}, bf16[1,128,4096]{2,1,0:T(8,128)(2,1)}, u32[]{:S(2)}) copy-start(bf16[1,128,4096]{2,1,0:T(8,128)(2,1)} %param.8) | copy-start | bytes 3145732
  2.5 1.2 %copy-start.1 = (bf16[1,128,4096]{2,1,0:T(8,128)(2,1)S(1)}, bf16[1,128,4096]{2,1,0:T(8,128)(2,1)}, u32[]{:S(2)}) copy-start(bf16[1,128,4096]{2,1,0:T(8,128)(2,1)} %param.9) | copy-start | bytes 3145732
  3.8 0.7 copy-start.2
  4.5 0.7 copy-start.3

commit v3 on v2

--- a/solution.py
+++ b/solution.py
@@ -33,6 +33,24 @@
 def layer(
     n_dp,
     n_seq,
+    rates_hbm,
+    q_hbm,
+    k_hbm,
+    v_hbm,
+    gain_hbm,
+    probe_hbm,
+    ends_hbm,
+    counts_hbm,
+    loss_ref,
+    gq_hbm,
+    gk_hbm,
+    gv_hbm,
+    ggain_ref,
+    gprobe_ref,
+    gq_ref,
+    gk_ref,
+    gv_ref,
+    save_sem,
     rates_ref,
     q_ref,
     k_ref,
@@ -41,12 +59,7 @@
     probe_ref,
     ends_ref,
     counts_ref,
-    loss_ref,
-    gq_ref,
-    gk_ref,
-    gv_ref,
-    ggain_ref,
-    gprobe_ref,
+    load_sem,
     state,
     peer,
     cin,
@@ -86,6 +99,22 @@
     send_s,
     recv_s,
 ):
+    loads = []
+    for at, (source, target) in enumerate(
+        (
+            (rates_hbm, rates_ref),
+            (k_hbm, k_ref),
+            (v_hbm, v_ref),
+            (ends_hbm, ends_ref),
+            (counts_hbm, counts_ref),
+            (gain_hbm, gain_ref),
+            (probe_hbm, probe_ref),
+            (q_hbm, q_ref),
+        )
+    ):
+        loads.append(pltpu.make_async_copy(source, target, load_sem.at[at]))
+        loads[-1].start()
+
     heads = rates_ref.shape[0]
     span = q_ref.shape[0]
     width = q_ref.shape[1] // heads
@@ -242,6 +271,8 @@
         swap(j, False).start()
         return carry
 
+    for load in loads[:3]:
+        load.wait()
     make_first(0, 0)
     edges = jnp.where(group > 0, 1, 0) + jnp.where(group < groups - 1, 1, 0)
     pl.semaphore_wait(barrier, len(exchanges) + edges)
@@ -254,6 +285,8 @@
             make_state(own + j * CHUNK + i)
 
     make_own(0)
+    for load in loads[3:]:
+        load.wait()
 
     steps = ends_ref.shape[1]
     position = seq * span + lax.broadcasted_iota(jnp.int32, (span, steps), 0)
@@ -404,10 +437,29 @@
             h = other + rel
             finish_back(h, gk_part[h], gv_part[h], btake[rel].astype(BF16))
 
+    def save(j):
+        if j == chunks:
+            part = pl.ds(pl.multiple_of(own * width, width), half * width)
+        else:
+            part = pl.ds(
+                pl.multiple_of((other + j * CHUNK) * width, width), CHUNK * width
+            )
+        return [
+            pltpu.make_async_copy(source.at[:, part], target.at[:, part], save_sem.at[at, j])
+            for at, (source, target) in enumerate(
+                ((gq_ref, gq_hbm), (gk_ref, gk_hbm), (gv_ref, gv_hbm))
+            )
+        ]
+
     total(0).start()
     for j in range(max(chunks, len(exchanges))):
         if j < chunks:
             backward_rest(j)
+            for saved in save(j):
+                saved.start()
+        if j == chunks - flight:
+            for saved in save(chunks):
+                saved.start()
         if j < len(exchanges):
             total(j).wait_recv()
             sums[j + 1] = sums[j] + sums_in[j]
@@ -420,6 +472,9 @@
     gprobe_ref[...] = summed * gain_ref[...]
     loss_ref[...] = sums[last, pl.ds(heads, 1), pl.ds(0, 1)]
 
+    for j in range(chunks + 1):
+        for saved in save(j):
+            saved.wait()
     for at in range(len(exchanges)):
         total(at).wait_send()
 
@@ -439,6 +494,20 @@
         return carry
 
     lax.fori_loop(0, chunks, drain, 0)
+
+
+def store(*refs):
+    sources, targets, held, sem_in, sem_out = refs[:6], refs[6:12], refs[12:18], refs[18], refs[19]
+    count = len(sources)
+    ins = [pltpu.make_async_copy(sources[n], held[n], sem_in.at[n]) for n in range(count)]
+    outs = [pltpu.make_async_copy(held[n], targets[n], sem_out.at[n]) for n in range(count)]
+    for copy in ins:
+        copy.start()
+    for n in range(count):
+        ins[n].wait()
+        outs[n].start()
+    for copy in outs:
+        copy.wait()
 
 
 def solution(mesh):
@@ -454,6 +523,7 @@
         width = features // heads
         half = heads // 2
         chunks = half // CHUNK
+        hbm = pl.BlockSpec(memory_space=pltpu.HBM)
         vmem = pl.BlockSpec(memory_space=pltpu.VMEM)
         rows = jax.ShapeDtypeStruct((span, features), BF16)
         table = jax.ShapeDtypeStruct((heads, width), F32)
@@ -463,12 +533,25 @@
                 pltpu.VMEM((half, width, width), F32)
             ] * 5
 
-        loss, gq, gk, gv, ggain, gprobe = pl.pallas_call(
+        results = pl.pallas_call(
             functools.partial(layer, n_dp, n_seq),
             out_shape=(jax.ShapeDtypeStruct((1, 1), F32), rows, rows, rows, table, table),
-            in_specs=[pl.BlockSpec(memory_space=pltpu.SMEM)] + [vmem] * 7,
-            out_specs=(vmem,) * 6,
-            scratch_shapes=scan_buffers()
+            in_specs=[hbm] * 8,
+            out_specs=(vmem, hbm, hbm, hbm, vmem, vmem),
+            scratch_shapes=[pltpu.VMEM((span, features), BF16)] * 3
+            + [
+                pltpu.SemaphoreType.DMA((3, chunks + 1)),
+                pltpu.SMEM((heads,), F32),
+                pltpu.VMEM((span, features), BF16),
+                pltpu.VMEM((span, features), BF16),
+                pltpu.VMEM((span, features), BF16),
+                pltpu.VMEM((heads, width), F32),
+                pltpu.VMEM((heads, width), F32),
+                pltpu.VMEM(step_ends.shape, jnp.int32),
+                pltpu.VMEM(step_counts.shape, jnp.int32),
+                pltpu.SemaphoreType.DMA((8,)),
+            ]
+            + scan_buffers()
             + scan_buffers()
             + [
                 pltpu.VMEM((heads, width, width), BF16),
@@ -487,7 +570,7 @@
             + [pltpu.SemaphoreType.DMA((chunks,))] * 12
             + [pltpu.SemaphoreType.DMA((exchanges,))] * 2,
             compiler_params=pltpu.CompilerParams(
-                collective_id=0, has_side_effects=True, vmem_limit_bytes=48 * 1024 * 1024
+                collective_id=0, has_side_effects=True, vmem_limit_bytes=60 * 1024 * 1024
             ),
             cost_estimate=pl.CostEstimate(
                 flops=28 * heads * span * width * width,
@@ -504,6 +587,15 @@
             step_ends,
             step_counts,
         )
+        loss, gq, gk, gv, ggain, gprobe = pl.pallas_call(
+            store,
+            out_shape=tuple(jax.ShapeDtypeStruct(a.shape, a.dtype) for a in results),
+            in_specs=[hbm] * 6,
+            out_specs=(hbm,) * 6,
+            scratch_shapes=[pltpu.VMEM(a.shape, a.dtype) for a in results]
+            + [pltpu.SemaphoreType.DMA((6,))] * 2,
+            compiler_params=pltpu.CompilerParams(vmem_limit_bytes=60 * 1024 * 1024),
+        )(*results)
         return (
             loss.reshape(()),
             gq[None],

time: 114 us -> 107 us (0.939)
  local copies, waits for them, and re-layouts: 8.67 us -> 0 us
  Pallas kernels: 102 us -> 106 us
  between operations: 2.36 us -> 0.64 us
    unnamed x19 -> x0, local copies, waits for them, and re-layouts: 8.67 us -> none
    pallas_call x0 -> x1, Pallas kernels: none -> 3.55 us  [on_device(): pl.pallas_call(store, out_shape=tuple((jax.ShapeDtypeStruct(a.shape, a.dt...]
where the time goes in v3:
time: 107 us
  Pallas kernels  106 us (99%)
    pallas_call x1, Pallas kernels, on_device(): pl.pallas_call(functools.partial(layer, n_dp, n_seq), out_shape=(jax.Shap...  102 us
    pallas_call x1, Pallas kernels, on_device(): pl.pallas_call(store, out_shape=tuple((jax.ShapeDtypeStruct(a.shape, a.dt...  3.55 us

profile of v3, /device:TPU:0, one launch (start us, length us, event | category | flops | bytes accessed | tf_op | source)
XLA Modules:
  0.0 106.7 jit_solution(12871119741076173051)
XLA Ops:
  0.6 102.5 %shard_map.127 = (f32[1,1]{1,0:T(1,128)}, bf16[128,4096]{1,0:T(8,128)(2,1)}, bf16[128,4096]{1,0:T(8,128)(2,1)}, bf16[128,4096]{1,0:T(8,128)(2,1)}, f32[32,128]{1,0:T(8,128)}, /*index=5*/f32[32,128]{1,0:T(8,128)}) custom-call(f32[32]{0:T(128)} %rates_hbm.1, bf16[128,4096]{1,0:T(8,128)(2,1)} %bitcast.11, bf16[128,4096]{1,0:T(8,128)(2,1)} %bitcast.12, ...), custom_call_target="tpu_custom_call" | custom-call | flops 1879048192 | bytes 6291456 | tf_op jit(solution)/shard_map/pallas_call | solution.py:536
  103.1 3.5 %shard_map.128 = (f32[1,1]{1,0:T(1,128)}, bf16[128,4096]{1,0:T(8,128)(2,1)}, bf16[128,4096]{1,0:T(8,128)(2,1)}, bf16[128,4096]{1,0:T(8,128)(2,1)}, f32[32,128]{1,0:T(8,128)}, /*index=5*/f32[32,128]{1,0:T(8,128)}) custom-call(f32[1,1]{1,0:T(1,128)} %get-tuple-element.18.refs_0_, bf16[128,4096]{1,0:T(8,128)(2,1)} %get-tuple-element.19.refs_1_, ...), custom_call_target="tpu_custom_call" | custom-call | tf_op jit(solution)/shard_map/pallas_call | solution.py:590
